TPU v7x, 32 devices: a whole 2x2x4 slice. The times are simulated.
32 devices in a mesh: groups: 2 (over x), tm: 16 (over z, y, core).
Axes of the slice: x: 2, y: 2, z: 4, core: 2. Of those that a mesh axis runs over, the one named last changes fastest.
Arguments:
- intensity: bfloat16 [64, 24576], P(('groups', 'tm')), parts along dimension 0, may hold values from 0.19921875 to 5
- cycle_label: int32 [49152], P('groups'), parts along dimension 0, may hold values from 0 to 71, as said below
- pixel_mask: int32 [49152], P('groups'), parts along dimension 0, may hold values from 0 to 1, as said below
- pair_table: int32 [16, 16], replicated, may hold values from 0 to 1, as said below
Outputs:
- two_time: float32 [64, 72, 32], P(('groups', 'tm')), parts along dimension 0
There are 2 independent parts, one for each index of `groups`. A program takes and returns all parts, laid end to end along the dimension named above; an argument that names none is the same for every part. Nothing has to cross between parts.
Inputs may be any that keep to these rules, and one draw needn't show every extreme that they name: `cycle_label`: pixel labels lie in 0 to 71; every cycle holds at least one live pixel. `pixel_mask`: every cycle holds at least one pixel whose mask is 1. `pair_table`: Symmetric, with ones on the diagonal.
All inputs are finite; a program needn't handle non-finite values.
Results may differ from a plain program's by a relative error of at most 0.0003.
Values may be sent and summed in bfloat16 or wider, within the bound.
A program may use at most 128 MiB of HBM per device.

v0:
```python
import functools

import jax
import jax.numpy as jnp
from jax import lax
from jax.experimental import pallas as pl
from jax.experimental.pallas import tpu as pltpu
from jax.sharding import PartitionSpec as P

CYCLES = 72
GROUPS8 = CYCLES // 8
LANES = 128
NT = (((1,), (1,)), ((), ()))


def member_of(label, mask):
    key = jnp.where(mask == 1, label, -1)
    ids = lax.broadcasted_iota(jnp.int32, (CYCLES, label.shape[1]), 0)
    return jnp.where(key == ids, 1.0, 0.0).astype(jnp.bfloat16)


def kernel(
    n, x_ref, label_ref, mask_ref, pair_ref, out_ref,
    pixels, frames32, part_out, part_in, stat_out, stat_in, stat_all, ones8, member_own,
    send1, recv1, send2, recv2, send3, recv3,
):
    me = lax.axis_index("tm")
    per, total = x_ref.shape
    share = total // n
    frames = n * per
    pack = max(LANES // frames, 1)

    def peer(step):
        sign = 1 - 2 * lax.rem(step, 2)
        return lax.rem(me + n // 2 + sign * ((step + 1) // 2) + n, n)

    def share_of(device):
        return pl.ds(pl.multiple_of(device * share, LANES), share)

    def pixel_copy(device, slot):
        return pltpu.make_async_remote_copy(
            src_ref=x_ref.at[:, share_of(device)],
            dst_ref=pixels.at[slot],
            send_sem=send1.at[device],
            recv_sem=recv1.at[slot],
            device_id={"tm": device},
            device_id_type=pl.DeviceIdType.MESH,
        )

    def stat_copy(device, slot):
        return pltpu.make_async_remote_copy(
            src_ref=stat_out,
            dst_ref=stat_in.at[slot],
            send_sem=send3.at[device],
            recv_sem=recv3.at[slot],
            device_id={"tm": device},
            device_id_type=pl.DeviceIdType.MESH,
        )

    def part_copy(device, slot):
        return pltpu.make_async_remote_copy(
            src_ref=part_out.at[device],
            dst_ref=part_in.at[slot],
            send_sem=send2.at[device],
            recv_sem=recv2.at[slot],
            device_id={"tm": device},
            device_id_type=pl.DeviceIdType.MESH,
        )

    barrier = pltpu.get_barrier_semaphore()

    def greet(step, _):
        pl.semaphore_signal(
            barrier, inc=1, device_id={"tm": peer(step)}, device_id_type=pl.DeviceIdType.MESH
        )
        return 0

    lax.fori_loop(0, n - 1, greet, 0)
    pl.semaphore_wait(barrier, n - 1)

    def send_pixels(step, _):
        pixel_copy(peer(step), me).start()
        return 0

    lax.fori_loop(0, n - 1, send_pixels, 0)

    pixels[me] = x_ref[:, share_of(me)]
    ones8[...] = jnp.ones_like(ones8)

    def local_sums(block, running):
        where = share_of(block)
        member = member_of(label_ref[:, where], mask_ref[:, where])
        ones8[:per] = x_ref[:, where].astype(jnp.float32)
        return running + lax.dot_general(
            ones8[...].astype(jnp.bfloat16), member, NT, preferred_element_type=jnp.float32
        )

    stats = lax.fori_loop(0, n, local_sums, jnp.zeros((8, CYCLES), jnp.float32))
    stat_out[...] = jnp.zeros_like(stat_out)
    stat_out[:, :CYCLES] = stats
    stat_in[me] = stat_out[...]

    def send_stats(step, _):
        stat_copy(peer(step), me).start()
        return 0

    lax.fori_loop(0, n - 1, send_stats, 0)

    member_own[...] = member_of(label_ref[:, share_of(me)], mask_ref[:, share_of(me)])

    def take_pixels(step, _):
        pixel_copy(peer(step), peer(step)).wait_recv()
        return 0

    lax.fori_loop(0, n - 1, take_pixels, 0)
    for device in range(n):
        frames32[device * per : (device + 1) * per] = pixels[device].astype(jnp.float32)
    right = frames32[...].astype(jnp.bfloat16)

    def partial(device):
        rows = pixels[device].astype(jnp.float32)
        grams = []
        for f in range(per):
            weighted = member_own[...] * rows[f : f + 1].astype(jnp.bfloat16)
            grams.append(lax.dot_general(weighted, right, NT, preferred_element_type=jnp.float32))
        tiles = [g[8 * c : 8 * c + 8] for g in grams for c in range(GROUPS8)]
        while len(tiles) % pack:
            tiles.append(jnp.zeros((8, frames), jnp.float32))
        return [jnp.concatenate(tiles[i : i + pack], axis=1) for i in range(0, len(tiles), pack)]

    def send_part(step, _):
        device = peer(step)
        for i, tile in enumerate(partial(device)):
            part_out[device, 8 * i : 8 * i + 8] = tile
        part_copy(device, me).start()
        return 0

    lax.fori_loop(0, n - 1, send_part, 0)
    for i, tile in enumerate(partial(me)):
        part_in[me, 8 * i : 8 * i + 8] = tile

    def take_stats(step, _):
        stat_copy(peer(step), peer(step)).wait_recv()
        return 0

    lax.fori_loop(0, n - 1, take_stats, 0)
    for device in range(n):
        stat_all[device * per : (device + 1) * per] = stat_in[device, :per]
    sums = jnp.transpose(stat_all[...])[:CYCLES]
    own = jnp.transpose(stat_out[...])[:CYCLES]
    blocks = lax.broadcasted_iota(jnp.int32, (n, frames), 0)
    owners = lax.broadcasted_iota(jnp.int32, (n, frames), 1) // per
    spread = jnp.where(blocks == owners, 1.0, 0.0)
    table = pair_ref[...].astype(jnp.float32)
    mine = jnp.where(lax.broadcasted_iota(jnp.int32, (n, n), 0) == me, table, 0.0)
    keep_row = jnp.sum(mine, axis=0, keepdims=True)
    keep = lax.dot_general(
        jnp.broadcast_to(keep_row, (8, n)).astype(jnp.bfloat16),
        spread.astype(jnp.bfloat16),
        (((1,), (0,)), ((), ())),
        preferred_element_type=jnp.float32,
    )[:1]
    counts = own[:, per : per + 1]
    factors = [counts * keep / (own[:, f : f + 1] * sums) for f in range(per)]

    def take_parts(step, _):
        part_copy(peer(step), peer(step)).wait_recv()
        return 0

    lax.fori_loop(0, n - 1, take_parts, 0)
    for i in range(part_in.shape[1] // 8):
        tile = part_in[0, 8 * i : 8 * i + 8]
        for device in range(1, n):
            tile = tile + part_in[device, 8 * i : 8 * i + 8]
        for b in range(pack):
            f, c = divmod(i * pack + b, GROUPS8)
            if f < per:
                gram = tile[:, b * frames : (b + 1) * frames]
                out_ref[f, 8 * c : 8 * c + 8] = gram * factors[f][8 * c : 8 * c + 8]

    def settle(step, _):
        pixel_copy(peer(step), me).wait_send()
        stat_copy(peer(step), me).wait_send()
        part_copy(peer(step), me).wait_send()
        return 0

    lax.fori_loop(0, n - 1, settle, 0)


def on_device(n, intensity, cycle_label, pixel_mask, pair_table):
    per, total = intensity.shape
    share = total // n
    frames = n * per
    pack = max(LANES // frames, 1)
    rows = -(-per * GROUPS8 // pack) * 8
    width = pack * frames
    vmem = pl.BlockSpec(memory_space=pltpu.VMEM)
    sems = pltpu.SemaphoreType.DMA((n,))
    return pl.pallas_call(
        functools.partial(kernel, n),
        out_shape=jax.ShapeDtypeStruct((per, CYCLES, frames), jnp.float32),
        in_specs=[vmem] * 4,
        out_specs=vmem,
        scratch_shapes=[
            pltpu.VMEM((n, per, share), jnp.bfloat16),
            pltpu.VMEM((frames, share), jnp.float32),
            pltpu.VMEM((n, rows, width), jnp.float32),
            pltpu.VMEM((n, rows, width), jnp.float32),
            pltpu.VMEM((8, LANES), jnp.float32),
            pltpu.VMEM((n, 8, LANES), jnp.float32),
            pltpu.VMEM((frames, LANES), jnp.float32),
            pltpu.VMEM((8, share), jnp.float32),
            pltpu.VMEM((CYCLES, share), jnp.bfloat16),
            sems, sems, sems, sems, sems, sems,
        ],
        compiler_params=pltpu.CompilerParams(
            collective_id=0, has_side_effects=True, vmem_limit_bytes=40 * 1024 * 1024
        ),
    )(intensity, cycle_label.reshape(1, total), pixel_mask.reshape(1, total), pair_table)


def solution(mesh):
    in_specs = (P(("groups", "tm"), None), P("groups"), P("groups"), P())
    out_specs = P(("groups", "tm"), None, None)
    return jax.shard_map(
        functools.partial(on_device, mesh.shape["tm"]),
        mesh=mesh, in_specs=in_specs, out_specs=out_specs, check_vma=False,
    )
```

profile of v0, /device:TPU:0, one launch (start us, length us, event | category | flops | bytes accessed | tf_op | source)
XLA Modules:
  0.0 25.4 jit_solution(16578809241159774087)
XLA Ops:
  0.0 0.0 copy-start
  0.0 0.9 %copy-done = bf16[2,24576]{1,0:T(2,128)(2,1)S(1)} copy-done((bf16[2,24576]{1,0:T(2,128)(2,1)S(1)}, bf16[2,24576]{1,0:T(2,128)(2,1)}, u32[]{:S(2)}) %copy-start) | copy-done | bytes 98328
  0.9 0.0 copy-start.1
  0.9 0.9 %copy-done.1 = s32[24576]{0:T(1024)S(1)} copy-done((s32[24576]{0:T(1024)S(1)}, s32[24576]{0:T(1024)}, u32[]{:S(2)}) %copy-start.1) | copy-done | bytes 98328
  1.8 0.0 copy-start.2
  1.8 0.9 %copy-done.2 = s32[24576]{0:T(1024)S(1)} copy-done((s32[24576]{0:T(1024)S(1)}, s32[24576]{0:T(1024)}, u32[]{:S(2)}) %copy-start.2) | copy-done | bytes 98328
  2.7 0.0 copy-start.3
  2.7 0.7 %copy-done.3 = s32[16,16]{1,0:T(8,128)S(1)} copy-done((s32[16,16]{1,0:T(8,128)S(1)}, s32[16,16]{1,0:T(8,128)}, u32[]{:S(2)}) %copy-start.3) | copy-done | bytes 1048
  3.4 21.3 %shard_map.46 = f32[2,72,32]{2,1,0:T(8,128)S(1)} custom-call(bf16[2,24576]{1,0:T(2,128)(2,1)S(1)} %copy-done, s32[1,24576]{1,0:T(1,128)S(1)} %bitcast.2, s32[1,24576]{1,0:T(1,128)S(1)} %bitcast.3, s32[16,16]{1,0:T(8,128)S(1)} %copy-done.3), custom_call_target="tpu_custom_call" | custom-call | tf_op jit(solution)/shard_map/pallas_call | solution.py:199
  24.7 0.7 %copy.5 = f32[2,72,32]{1,2,0:T(8,128)} copy(f32[2,72,32]{2,1,0:T(8,128)S(1)} %shard_map.46) | data formatting | bytes 36864 | tf_op jit(solution)/shard_map/pallas_call | solution.py:199
Async XLA Ops:
  0.0 0.9 %copy-start = (bf16[2,24576]{1,0:T(2,128)(2,1)S(1)}, bf16[2,24576]{1,0:T(2,128)(2,1)}, u32[]{:S(2)}) copy-start(bf16[2,24576]{1,0:T(2,128)(2,1)} %x_ref.1) | copy-start | bytes 294916
  0.9 0.9 %copy-start.1 = (s32[24576]{0:T(1024)S(1)}, s32[24576]{0:T(1024)}, u32[]{:S(2)}) copy-start(s32[24576]{0:T(1024)} %param.5) | copy-start | bytes 294916
  1.8 0.9 %copy-start.2 = (s32[24576]{0:T(1024)S(1)}, s32[24576]{0:T(1024)}, u32[]{:S(2)}) copy-start(s32[24576]{0:T(1024)} %param.6) | copy-start | bytes 294916
  2.7 0.7 %copy-start.3 = (s32[16,16]{1,0:T(8,128)S(1)}, s32[16,16]{1,0:T(8,128)}, u32[]{:S(2)}) copy-start(s32[16,16]{1,0:T(8,128)} %pair_ref.1) | copy-start | bytes 3076
where the time goes:
time: 25.6 us; the launch traced here: 25.4 us
  Pallas kernels  21.3 us (83%)
  local copies, waits for them, and re-layouts  4.06 us (16%)
    pallas_call x1, Pallas kernels, on_device(): pl.pallas_call(functools.partial(kernel, n), out_shape=jax.ShapeDtypeStru...  21.3 us
    unnamed x8, local copies, waits for them, and re-layouts  3.37 us
    pallas_call x1, local copies, waits for them, and re-layouts, on_device(): pl.pallas_call(functools.partial(kernel, n), out_shape=jax.ShapeDtypeStru...  0.69 us

commit v1 on v0

--- a/solution.py
+++ b/solution.py
@@ -20,29 +20,33 @@
 
 
 def kernel(
-    n, x_ref, label_ref, mask_ref, pair_ref, out_ref,
-    pixels, frames32, part_out, part_in, stat_out, stat_in, stat_all, ones8, member_own,
-    send1, recv1, send2, recv2, send3, recv3,
+    n, x_hbm, label_hbm, mask_hbm, pair_hbm, out_ref,
+    x_ref, label_ref, mask_ref, pair_ref, pixels, frames32, part_out, part_in, stat_out, stat_in, stat_all, ones8, member_own,
+    load, send1, recv1, send2, recv2, send3, recv3,
 ):
     me = lax.axis_index("tm")
-    per, total = x_ref.shape
+    per, total = x_hbm.shape
     share = total // n
     frames = n * per
     pack = max(LANES // frames, 1)
 
     def peer(step):
-        sign = 1 - 2 * lax.rem(step, 2)
-        return lax.rem(me + n // 2 + sign * ((step + 1) // 2) + n, n)
+        there = me + step
+        return jnp.where(there >= n, there - n, there)
+
+    def all_of(buffer, sem):
+        blocks = buffer.at[pl.ds(0, n - 1)]
+        pltpu.make_async_copy(blocks, blocks, sem).wait()
 
     def share_of(device):
         return pl.ds(pl.multiple_of(device * share, LANES), share)
 
     def pixel_copy(device, slot):
         return pltpu.make_async_remote_copy(
-            src_ref=x_ref.at[:, share_of(device)],
+            src_ref=x_hbm.at[:, share_of(device)],
             dst_ref=pixels.at[slot],
-            send_sem=send1.at[device],
-            recv_sem=recv1.at[slot],
+            send_sem=send1,
+            recv_sem=recv1,
             device_id={"tm": device},
             device_id_type=pl.DeviceIdType.MESH,
         )
@@ -51,8 +55,8 @@
         return pltpu.make_async_remote_copy(
             src_ref=stat_out,
             dst_ref=stat_in.at[slot],
-            send_sem=send3.at[device],
-            recv_sem=recv3.at[slot],
+            send_sem=send3,
+            recv_sem=recv3,
             device_id={"tm": device},
             device_id_type=pl.DeviceIdType.MESH,
         )
@@ -61,28 +65,31 @@
         return pltpu.make_async_remote_copy(
             src_ref=part_out.at[device],
             dst_ref=part_in.at[slot],
-            send_sem=send2.at[device],
-            recv_sem=recv2.at[slot],
+            send_sem=send2,
+            recv_sem=recv2,
             device_id={"tm": device},
             device_id_type=pl.DeviceIdType.MESH,
         )
 
+    loads = [
+        pltpu.make_async_copy(source, target, load.at[i])
+        for i, (source, target) in enumerate(
+            [(label_hbm, label_ref), (mask_hbm, mask_ref), (x_hbm, x_ref), (pair_hbm, pair_ref)]
+        )
+    ]
+    for copy in loads:
+        copy.start()
     barrier = pltpu.get_barrier_semaphore()
 
-    def greet(step, _):
+    for step in range(1, n):
         pl.semaphore_signal(
             barrier, inc=1, device_id={"tm": peer(step)}, device_id_type=pl.DeviceIdType.MESH
         )
-        return 0
-
-    lax.fori_loop(0, n - 1, greet, 0)
     pl.semaphore_wait(barrier, n - 1)
-
-    def send_pixels(step, _):
+    for step in range(1, n):
         pixel_copy(peer(step), me).start()
-        return 0
-
-    lax.fori_loop(0, n - 1, send_pixels, 0)
+    for copy in loads:
+        copy.wait()
 
     pixels[me] = x_ref[:, share_of(me)]
     ones8[...] = jnp.ones_like(ones8)
@@ -99,20 +106,13 @@
     stat_out[...] = jnp.zeros_like(stat_out)
     stat_out[:, :CYCLES] = stats
     stat_in[me] = stat_out[...]
-
-    def send_stats(step, _):
+    member_own[...] = member_of(label_ref[:, share_of(me)], mask_ref[:, share_of(me)])
+
+
+    for step in range(1, n):
         stat_copy(peer(step), me).start()
-        return 0
-
-    lax.fori_loop(0, n - 1, send_stats, 0)
-
-    member_own[...] = member_of(label_ref[:, share_of(me)], mask_ref[:, share_of(me)])
-
-    def take_pixels(step, _):
-        pixel_copy(peer(step), peer(step)).wait_recv()
-        return 0
-
-    lax.fori_loop(0, n - 1, take_pixels, 0)
+
+    all_of(pixels, recv1)
     for device in range(n):
         frames32[device * per : (device + 1) * per] = pixels[device].astype(jnp.float32)
     right = frames32[...].astype(jnp.bfloat16)
@@ -135,15 +135,11 @@
         part_copy(device, me).start()
         return 0
 
-    lax.fori_loop(0, n - 1, send_part, 0)
+    lax.fori_loop(1, n, send_part, 0)
     for i, tile in enumerate(partial(me)):
         part_in[me, 8 * i : 8 * i + 8] = tile
 
-    def take_stats(step, _):
-        stat_copy(peer(step), peer(step)).wait_recv()
-        return 0
-
-    lax.fori_loop(0, n - 1, take_stats, 0)
+    all_of(stat_in, recv3)
     for device in range(n):
         stat_all[device * per : (device + 1) * per] = stat_in[device, :per]
     sums = jnp.transpose(stat_all[...])[:CYCLES]
@@ -163,11 +159,7 @@
     counts = own[:, per : per + 1]
     factors = [counts * keep / (own[:, f : f + 1] * sums) for f in range(per)]
 
-    def take_parts(step, _):
-        part_copy(peer(step), peer(step)).wait_recv()
-        return 0
-
-    lax.fori_loop(0, n - 1, take_parts, 0)
+    all_of(part_in, recv2)
     for i in range(part_in.shape[1] // 8):
         tile = part_in[0, 8 * i : 8 * i + 8]
         for device in range(1, n):
@@ -178,13 +170,9 @@
                 gram = tile[:, b * frames : (b + 1) * frames]
                 out_ref[f, 8 * c : 8 * c + 8] = gram * factors[f][8 * c : 8 * c + 8]
 
-    def settle(step, _):
-        pixel_copy(peer(step), me).wait_send()
-        stat_copy(peer(step), me).wait_send()
-        part_copy(peer(step), me).wait_send()
-        return 0
-
-    lax.fori_loop(0, n - 1, settle, 0)
+    all_of(pixels, send1)
+    all_of(stat_in, send3)
+    all_of(part_in, send2)
 
 
 def on_device(n, intensity, cycle_label, pixel_mask, pair_table):
@@ -195,13 +183,17 @@
     rows = -(-per * GROUPS8 // pack) * 8
     width = pack * frames
     vmem = pl.BlockSpec(memory_space=pltpu.VMEM)
-    sems = pltpu.SemaphoreType.DMA((n,))
+    sem = pltpu.SemaphoreType.DMA
     return pl.pallas_call(
         functools.partial(kernel, n),
         out_shape=jax.ShapeDtypeStruct((per, CYCLES, frames), jnp.float32),
-        in_specs=[vmem] * 4,
+        in_specs=[pl.BlockSpec(memory_space=pl.ANY)] * 4,
         out_specs=vmem,
         scratch_shapes=[
+            pltpu.VMEM((per, total), jnp.bfloat16),
+            pltpu.VMEM((1, total), jnp.int32),
+            pltpu.VMEM((1, total), jnp.int32),
+            pltpu.VMEM(pair_table.shape, jnp.int32),
             pltpu.VMEM((n, per, share), jnp.bfloat16),
             pltpu.VMEM((frames, share), jnp.float32),
             pltpu.VMEM((n, rows, width), jnp.float32),
@@ -211,10 +203,11 @@
             pltpu.VMEM((frames, LANES), jnp.float32),
             pltpu.VMEM((8, share), jnp.float32),
             pltpu.VMEM((CYCLES, share), jnp.bfloat16),
-            sems, sems, sems, sems, sems, sems,
+            pltpu.SemaphoreType.DMA((4,)),
+            sem, sem, sem, sem, sem, sem,
         ],
         compiler_params=pltpu.CompilerParams(
-            collective_id=0, has_side_effects=True, vmem_limit_bytes=40 * 1024 * 1024
+            collective_id=0, has_side_effects=True, vmem_limit_bytes=56 * 1024 * 1024
         ),
     )(intensity, cycle_label.reshape(1, total), pixel_mask.reshape(1, total), pair_table)
 

time: 25.6 us -> 21.6 us (0.84)
  local copies, waits for them, and re-layouts: 4.06 us -> 1.57 us
  Pallas kernels: 21.3 us -> 19.8 us
    unnamed x8 -> x0, local copies, waits for them, and re-layouts: 3.37 us -> none
    pallas_call x1, Pallas kernels: 21.3 us -> 19.8 us  [on_device(): pl.pallas_call(functools.partial(kernel, n), out_shape=jax.ShapeDtypeStru...]
    pallas_call x1, local copies, waits for them, and re-layouts: 0.69 us -> 1.57 us  [on_device(): pl.pallas_call(functools.partial(kernel, n), out_shape=jax.ShapeDtypeStru...]
where the time goes in v1:
time: 21.6 us; the launch traced here: 21.3 us
  Pallas kernels  19.8 us (92%)
  local copies, waits for them, and re-layouts  1.57 us (7%)
    pallas_call x1, Pallas kernels, on_device(): pl.pallas_call(functools.partial(kernel, n), out_shape=jax.ShapeDtypeStru...  19.8 us
    pallas_call x1, local copies, waits for them, and re-layouts, on_device(): pl.pallas_call(functools.partial(kernel, n), out_shape=jax.ShapeDtypeStru...  1.57 us

profile of v1, /device:TPU:0, one launch (start us, length us, event | category | flops | bytes accessed | tf_op | source)
XLA Modules:
  0.0 21.3 jit_solution(13341219742391347681)
XLA Ops:
  0.0 19.8 %shard_map.46 = f32[2,72,32]{2,1,0:T(8,128)} custom-call(bf16[2,24576]{1,0:T(2,128)(2,1)} %x_hbm.1, s32[1,24576]{1,0:T(1,128)} %bitcast.2, s32[1,24576]{1,0:T(1,128)} %bitcast.3, s32[16,16]{1,0:T(8,128)} %pair_hbm.1), custom_call_target="tpu_custom_call" | custom-call | tf_op jit(solution)/shard_map/pallas_call | solution.py:187
  19.8 1.6 %copy.5 = f32[2,72,32]{1,2,0:T(8,128)} copy(f32[2,72,32]{2,1,0:T(8,128)} %shard_map.46) | data formatting | bytes 36864 | tf_op jit(solution)/shard_map/pallas_call | solution.py:187

commit v2 on v1

--- a/solution.py
+++ b/solution.py
@@ -26,24 +26,34 @@
 ):
     me = lax.axis_index("tm")
     per, total = x_hbm.shape
-    share = total // n
+    half = n // 2
+    share = total // half
     frames = n * per
     pack = max(LANES // frames, 1)
+    base = jnp.where(me >= half, half, 0)
+    place = me - base
 
     def peer(step):
         there = me + step
         return jnp.where(there >= n, there - n, there)
 
+    def place_of(device):
+        return jnp.where(device >= half, device - half, device)
+
+    def mate(step):
+        there = place + step
+        return jnp.where(there >= half, there - half, there)
+
     def all_of(buffer, sem):
-        blocks = buffer.at[pl.ds(0, n - 1)]
+        blocks = buffer.at[pl.ds(0, buffer.shape[0] - 1)]
         pltpu.make_async_copy(blocks, blocks, sem).wait()
 
-    def share_of(device):
-        return pl.ds(pl.multiple_of(device * share, LANES), share)
+    def share_of(block):
+        return pl.ds(pl.multiple_of(block * share, LANES), share)
 
     def pixel_copy(device, slot):
         return pltpu.make_async_remote_copy(
-            src_ref=x_hbm.at[:, share_of(device)],
+            src_ref=x_hbm.at[:, share_of(place_of(device))],
             dst_ref=pixels.at[slot],
             send_sem=send1,
             recv_sem=recv1,
@@ -61,13 +71,13 @@
             device_id_type=pl.DeviceIdType.MESH,
         )
 
-    def part_copy(device, slot):
+    def part_copy(there):
         return pltpu.make_async_remote_copy(
-            src_ref=part_out.at[device],
-            dst_ref=part_in.at[slot],
+            src_ref=part_out.at[there],
+            dst_ref=part_in.at[place],
             send_sem=send2,
             recv_sem=recv2,
-            device_id={"tm": device},
+            device_id={"tm": base + there},
             device_id_type=pl.DeviceIdType.MESH,
         )
 
@@ -91,7 +101,7 @@
     for copy in loads:
         copy.wait()
 
-    pixels[me] = x_ref[:, share_of(me)]
+    pixels[me] = x_ref[:, share_of(place)]
     ones8[...] = jnp.ones_like(ones8)
 
     def local_sums(block, running):
@@ -102,11 +112,11 @@
             ones8[...].astype(jnp.bfloat16), member, NT, preferred_element_type=jnp.float32
         )
 
-    stats = lax.fori_loop(0, n, local_sums, jnp.zeros((8, CYCLES), jnp.float32))
+    stats = lax.fori_loop(0, half, local_sums, jnp.zeros((8, CYCLES), jnp.float32))
     stat_out[...] = jnp.zeros_like(stat_out)
     stat_out[:, :CYCLES] = stats
     stat_in[me] = stat_out[...]
-    member_own[...] = member_of(label_ref[:, share_of(me)], mask_ref[:, share_of(me)])
+    member_own[...] = member_of(label_ref[:, share_of(place)], mask_ref[:, share_of(place)])
 
 
     for step in range(1, n):
@@ -128,16 +138,23 @@
             tiles.append(jnp.zeros((8, frames), jnp.float32))
         return [jnp.concatenate(tiles[i : i + pack], axis=1) for i in range(0, len(tiles), pack)]
 
-    def send_part(step, _):
-        device = peer(step)
-        for i, tile in enumerate(partial(device)):
-            part_out[device, 8 * i : 8 * i + 8] = tile
-        part_copy(device, me).start()
+    def send_parts(places):
+        for there in places:
+            for i, tile in enumerate(partial(base + there)):
+                part_out[there, 8 * i : 8 * i + 8] = tile
+        for there in places:
+            part_copy(there).start()
+
+    def send_pair(pair, _):
+        send_parts([mate(2 * pair + 1), mate(2 * pair + 2)])
         return 0
 
-    lax.fori_loop(1, n, send_part, 0)
+    pairs = (half - 1) // 2
+    lax.fori_loop(0, pairs, send_pair, 0, unroll=pairs if half <= 8 else 1)
+    if (half - 1) % 2:
+        send_parts([mate(half - 1)])
     for i, tile in enumerate(partial(me)):
-        part_in[me, 8 * i : 8 * i + 8] = tile
+        part_in[place, 8 * i : 8 * i + 8] = tile
 
     all_of(stat_in, recv3)
     for device in range(n):
@@ -162,7 +179,7 @@
     all_of(part_in, recv2)
     for i in range(part_in.shape[1] // 8):
         tile = part_in[0, 8 * i : 8 * i + 8]
-        for device in range(1, n):
+        for device in range(1, half):
             tile = tile + part_in[device, 8 * i : 8 * i + 8]
         for b in range(pack):
             f, c = divmod(i * pack + b, GROUPS8)
@@ -177,7 +194,7 @@
 
 def on_device(n, intensity, cycle_label, pixel_mask, pair_table):
     per, total = intensity.shape
-    share = total // n
+    share = total // (n // 2)
     frames = n * per
     pack = max(LANES // frames, 1)
     rows = -(-per * GROUPS8 // pack) * 8
@@ -196,8 +213,8 @@
             pltpu.VMEM(pair_table.shape, jnp.int32),
             pltpu.VMEM((n, per, share), jnp.bfloat16),
             pltpu.VMEM((frames, share), jnp.float32),
-            pltpu.VMEM((n, rows, width), jnp.float32),
-            pltpu.VMEM((n, rows, width), jnp.float32),
+            pltpu.VMEM((n // 2, rows, width), jnp.float32),
+            pltpu.VMEM((n // 2, rows, width), jnp.float32),
             pltpu.VMEM((8, LANES), jnp.float32),
             pltpu.VMEM((n, 8, LANES), jnp.float32),
             pltpu.VMEM((frames, LANES), jnp.float32),

time: 21.6 us -> 19.5 us (0.903)
  Pallas kernels: 19.8 us -> 17.8 us
    pallas_call x1, Pallas kernels: 19.8 us -> 17.8 us  [on_device(): pl.pallas_call(functools.partial(kernel, n), out_shape=jax.ShapeDtypeStru...]
where the time goes in v2:
time: 19.5 us; the launch traced here: 19.4 us
  Pallas kernels  17.8 us (91%)
  local copies, waits for them, and re-layouts  1.57 us (8%)
    pallas_call x1, Pallas kernels, on_device(): pl.pallas_call(functools.partial(kernel, n), out_shape=jax.ShapeDtypeStru...  17.8 us
    pallas_call x1, local copies, waits for them, and re-layouts, on_device(): pl.pallas_call(functools.partial(kernel, n), out_shape=jax.ShapeDtypeStru...  1.57 us

profile of v2, /device:TPU:0, one launch (start us, length us, event | category | flops | bytes accessed | tf_op | source)
XLA Modules:
  0.0 19.4 jit_solution(17194168704273832010)
XLA Ops:
  0.0 17.8 %shard_map.46 = f32[2,72,32]{2,1,0:T(8,128)} custom-call(bf16[2,24576]{1,0:T(2,128)(2,1)} %x_hbm.1, s32[1,24576]{1,0:T(1,128)} %bitcast.2, s32[1,24576]{1,0:T(1,128)} %bitcast.3, s32[16,16]{1,0:T(8,128)} %pair_hbm.1), custom_call_target="tpu_custom_call" | custom-call | tf_op jit(solution)/shard_map/pallas_call | solution.py:204
  17.8 1.6 %copy.5 = f32[2,72,32]{1,2,0:T(8,128)} copy(f32[2,72,32]{2,1,0:T(8,128)} %shard_map.46) | data formatting | bytes 36864 | tf_op jit(solution)/shard_map/pallas_call | solution.py:204

commit v3 on v2

--- a/solution.py
+++ b/solution.py
@@ -53,7 +53,7 @@
 
     def pixel_copy(device, slot):
         return pltpu.make_async_remote_copy(
-            src_ref=x_hbm.at[:, share_of(place_of(device))],
+            src_ref=x_ref.at[:, share_of(place_of(device))],
             dst_ref=pixels.at[slot],
             send_sem=send1,
             recv_sem=recv1,
@@ -95,11 +95,11 @@
         pl.semaphore_signal(
             barrier, inc=1, device_id={"tm": peer(step)}, device_id_type=pl.DeviceIdType.MESH
         )
+    for copy in loads:
+        copy.wait()
     pl.semaphore_wait(barrier, n - 1)
     for step in range(1, n):
         pixel_copy(peer(step), me).start()
-    for copy in loads:
-        copy.wait()
 
     pixels[me] = x_ref[:, share_of(place)]
     ones8[...] = jnp.ones_like(ones8)

time: 19.5 us -> 19.4 us (level)
  Pallas kernels: 17.8 us -> 17.6 us
    pallas_call x1, Pallas kernels: 17.8 us -> 17.6 us  [on_device(): pl.pallas_call(functools.partial(kernel, n), out_shape=jax.ShapeDtypeStru...]
where the time goes in v3:
time: 19.4 us; the launch traced here: 19.2 us
  Pallas kernels  17.6 us (91%)
  local copies, waits for them, and re-layouts  1.57 us (8%)
    pallas_call x1, Pallas kernels, on_device(): pl.pallas_call(functools.partial(kernel, n), out_shape=jax.ShapeDtypeStru...  17.6 us
    pallas_call x1, local copies, waits for them, and re-layouts, on_device(): pl.pallas_call(functools.partial(kernel, n), out_shape=jax.ShapeDtypeStru...  1.57 us

profile of v3, /device:TPU:0, one launch (start us, length us, event | category | flops | bytes accessed | tf_op | source)
XLA Modules:
  0.0 19.2 jit_solution(2254995785152722004)
XLA Ops:
  0.0 17.6 %shard_map.46 = f32[2,72,32]{2,1,0:T(8,128)} custom-call(bf16[2,24576]{1,0:T(2,128)(2,1)} %x_hbm.1, s32[1,24576]{1,0:T(1,128)} %bitcast.2, s32[1,24576]{1,0:T(1,128)} %bitcast.3, s32[16,16]{1,0:T(8,128)} %pair_hbm.1), custom_call_target="tpu_custom_call" | custom-call | tf_op jit(solution)/shard_map/pallas_call | solution.py:204
  17.6 1.6 %copy.5 = f32[2,72,32]{1,2,0:T(8,128)} copy(f32[2,72,32]{2,1,0:T(8,128)} %shard_map.46) | data formatting | bytes 36864 | tf_op jit(solution)/shard_map/pallas_call | solution.py:204
